TPU v7x, 512 devices: a whole 4x4x16 slice. The times are simulated.
512 devices in a mesh: section: 4 (over x), replica: 16 (over z_lo, y), expert: 8 (over z_hi, core).
Axes of the slice: x: 4, y: 4, z: 16 (z_hi: 4, z_lo: 4; z = z_hi * 4 + z_lo), core: 2. Of those that a mesh axis runs over, the one named last changes fastest.
Arguments:
- tokens: bfloat16 [3, 256, 1536], P(None, 'replica'), may hold values from -6 to 6
- attn_gain: float32 [4, 1536], P('section'), may hold values from 0.25 to 1.75
- w_query: bfloat16 [4, 1536, 2048], P('section', None, 'expert'), may hold values from -0.15625 to 0.15625
- w_keyval: bfloat16 [4, 1536, 8, 128], P('section', None, 'expert'), may hold values from -0.15625 to 0.15625
- sinks: float32 [4, 32], P('section', 'expert'), may hold values from -2 to 260
- w_out: bfloat16 [4, 2048, 1536], P('section', 'expert'), may hold values from -0.125 to 0.125
- ffn_gain: float32 [4, 1536], P('section'), may hold values from 0.25 to 1.75
- router: bfloat16 [4, 1536, 16], P('section'), may hold values from -0.15625 to 0.15625
- w_gate_up: bfloat16 [4, 16, 2, 1536, 2048], P('section', 'replica', None, None, 'expert'), may hold values from -0.15625 to 0.15625
- w_down: bfloat16 [4, 16, 2048, 1536], P('section', 'replica', 'expert'), may hold values from -0.125 to 0.125
- kv_pool: bfloat16 [4, 2048, 16, 8, 128], P('section', 'replica', None, 'expert'), may hold values from -6 to 6
- block_table: int32 [256, 8], P('replica'), may hold values from 0 to 127, as said below
- lengths: int32 [256], P('replica'), may hold values from 1 to 128, as said below
- expert_ids: int32 [4, 3, 256, 4], P('section', None, 'replica'), may hold values from 0 to 15, all different within a row; in each aligned block of 16 rows (0 to 15, 16 to 31, ..., all dimensions but the last counted through in order) at most 5 rows name the same one
Outputs:
- layer_out: bfloat16 [4, 3, 256, 1536], P('section', None, 'replica', 'expert')
- fresh_kv: bfloat16 [4, 3, 256, 8, 128], P('section', None, 'replica', 'expert')
Inputs may be any that keep to these rules, and one draw needn't show every extreme that they name: `block_table`: rows 0 to 11 of each replica are its own requests and index its own pool; its last 4 rows are requests taken over from the replica before it (replica 0 from the last one) and index that replica's pool. All blocks named in one pool are different. `lengths`: some request has exactly 128 cached tokens. `expert_ids`: A row names 4 different experts. For each layer and step, at most 5 of one replica's 16 rows name the same expert, and that count is reached.
All inputs are finite; a program needn't handle non-finite values.
Results may differ from a plain program's by a relative error of at most 0.027.
Values may be sent and summed in bfloat16 or wider, within the bound.
A program may use at most 64 MiB of HBM per device.

v0:
```python
import jax
import jax.numpy as jnp
from jax import lax
from jax.sharding import PartitionSpec as P

MIG = 4


EPS = 1e-05
THETA = 150000.0
NEG = -1e30


def shifted(shard, axis, by):
    length = lax.axis_size(axis)
    return lax.ppermute(shard, axis, [(i, (i + by) % length) for i in range(length)])


def shifted_2(value, axis, steps):
    count = lax.axis_size(axis)
    leading, last = (max(0, -steps), min(count, count - steps))
    return lax.ppermute(value, axis, [(source, source + steps) for source in range(leading, last)])


def normed(values, gain):
    wide = values.astype(jnp.float32)
    mean_sq = jnp.mean(wide * wide, axis=-1, keepdims=True)
    return (wide * lax.rsqrt(mean_sq + EPS) * gain).astype(jnp.bfloat16)


def rotated(vectors, places):
    half = vectors.shape[-1] // 2
    freq = THETA ** (-2.0 * jnp.arange(half).astype(jnp.float32) / vectors.shape[-1])
    angle = places.astype(jnp.float32)[:, None] * freq[None, :]
    cosine = jnp.cos(angle)[:, None, :]
    sine = jnp.sin(angle)[:, None, :]
    first = vectors[..., :half]
    second = vectors[..., half:]
    return jnp.concatenate(
        [first * cosine - second * sine, second * cosine + first * sine], axis=-1
    )


def attend(query, cache, live_len, fresh, step_at, sink):
    head_dim = query.shape[-1]
    scale = head_dim ** (-0.5)
    past_keys = cache[..., :head_dim]
    past_vals = cache[..., head_dim:]
    score = (
        jnp.einsum("rkgd,rckd->rkgc", query, past_keys, preferred_element_type=jnp.float32) * scale
    )
    live = jnp.arange(cache.shape[1])[None, :] < live_len[:, None]
    score = jnp.where(live[:, None, None, :], score, NEG)
    new_keys = fresh[..., :head_dim]
    new_vals = fresh[..., head_dim:]
    recent = (
        jnp.einsum("rkgd,srkd->rkgs", query, new_keys, preferred_element_type=jnp.float32) * scale
    )
    seen = jnp.arange(fresh.shape[0]) <= step_at
    recent = jnp.where(seen[None, None, None, :], recent, NEG)
    peak = jnp.maximum(jnp.maximum(jnp.max(score, -1), jnp.max(recent, -1)), sink[None])
    past_w = jnp.exp(score - peak[..., None])
    new_w = jnp.exp(recent - peak[..., None])
    total = jnp.sum(past_w, -1) + jnp.sum(new_w, -1) + jnp.exp(sink[None] - peak)
    past_b = (past_w / total[..., None]).astype(jnp.bfloat16)
    new_b = (new_w / total[..., None]).astype(jnp.bfloat16)
    merged = jnp.einsum("rkgc,rckd->rkgd", past_b, past_vals, preferred_element_type=jnp.float32)
    merged = merged + jnp.einsum(
        "rkgs,srkd->rkgd", new_b, new_vals, preferred_element_type=jnp.float32
    )
    return merged.astype(jnp.bfloat16)


def local(
    tokens,
    attn_gain,
    w_query,
    w_keyval,
    sinks,
    w_out,
    ffn_gain,
    router,
    w_gate_up,
    w_down,
    kv_pool,
    block_table,
    lengths,
    expert_ids,
):
    step_count, row_count, model_width = tokens.shape
    expert_count = router.shape[2]
    kv_local = w_keyval.shape[2]
    pair_width = w_keyval.shape[3]
    head_dim = pair_width // 2
    q_local = sinks.shape[1]
    group = q_local // kv_local
    choose_count = expert_ids.shape[3]
    part_count = lax.axis_size("expert")
    share_width = model_width // part_count
    slot_cap = min(
        row_count, (5 * row_count * choose_count + 4 * expert_count - 1) // (4 * expert_count)
    )
    section_index = lax.axis_index("section")
    lane_index = lax.axis_index("expert")
    section_count = lax.axis_size("section")
    own_pool = kv_pool[0]
    block_count = block_table.shape[1]
    depth = block_count * own_pool.shape[1]
    staying = row_count - MIG
    wanted = shifted(block_table[staying:], "replica", -1)
    leaving = own_pool[wanted.reshape(-1)]
    arrived = shifted(leaving, "replica", 1)
    resident = own_pool[block_table[:staying].reshape(-1)]
    cache = jnp.concatenate([resident, arrived], axis=0).reshape(
        row_count, depth, kv_local, pair_width
    )
    query_weight = w_query[0]
    keyval_weight = w_keyval[0].reshape(model_width, kv_local * pair_width)
    out_weight = w_out[0]
    sink_local = sinks[0].reshape(kv_local, group)
    router_weight = router[0]
    gate_up = w_gate_up[0, 0]
    down_weight = w_down[0, 0]
    expert_range = jnp.arange(expert_count)
    slot_range = jnp.arange(expert_count * slot_cap)
    fresh = jnp.zeros((step_count, row_count, kv_local, pair_width), jnp.bfloat16)
    results = jnp.zeros((step_count, row_count, share_width), jnp.bfloat16)
    incoming = None
    tick_total = step_count + section_count - 1
    for tick_index in range(tick_total):
        offset = tick_index - section_index
        active = (offset >= 0) & (offset < step_count)
        step_at = jnp.clip(offset, 0, step_count - 1)
        first_input = lax.dynamic_index_in_dim(tokens, step_at, 0, keepdims=False)
        if tick_index == 0:
            current = first_input
        else:
            current = jnp.where(section_index == 0, first_input, incoming)
        places = lengths + step_at
        normal_in = normed(current, attn_gain[0])
        query = jnp.dot(normal_in, query_weight, preferred_element_type=jnp.float32).reshape(
            row_count, q_local, head_dim
        )
        query = (
            rotated(query, places)
            .astype(jnp.bfloat16)
            .reshape(row_count, kv_local, group, head_dim)
        )
        keyval = jnp.dot(normal_in, keyval_weight, preferred_element_type=jnp.float32).reshape(
            row_count, kv_local, pair_width
        )
        new_entry = jnp.concatenate(
            [rotated(keyval[..., :head_dim], places), keyval[..., head_dim:]], axis=-1
        ).astype(jnp.bfloat16)
        fresh_now = fresh.at[step_at].set(new_entry)
        attended = attend(query, cache, lengths, fresh_now, step_at, sink_local).reshape(
            row_count, q_local * head_dim
        )
        mixed = lax.psum(
            jnp.dot(attended, out_weight, preferred_element_type=jnp.float32).astype(jnp.bfloat16),
            "expert",
        ).astype(jnp.float32)
        after_attn = (current.astype(jnp.float32) + mixed).astype(jnp.bfloat16)
        mlp_in = normed(after_attn, ffn_gain[0])
        logits = jnp.dot(mlp_in, router_weight, preferred_element_type=jnp.float32)
        chosen = lax.dynamic_index_in_dim(expert_ids[0], step_at, 0, keepdims=False)
        chosen_hot = chosen[:, :, None] == expert_range[None, None, :]
        gates = jax.nn.sigmoid(jnp.sum(jnp.where(chosen_hot, logits[:, None, :], 0.0), -1))
        weight = gates / jnp.sum(gates, -1, keepdims=True)
        flat_hot = chosen_hot.reshape(row_count * choose_count, expert_count).astype(jnp.int32)
        earlier = jnp.cumsum(flat_hot, axis=0) - flat_hot
        slot_of = jnp.sum(earlier * flat_hot, -1)
        target = chosen.reshape(-1) * slot_cap + slot_of
        placing = jnp.any(
            slot_range[:, None, None] == target.reshape(row_count, choose_count)[None], -1
        ).astype(jnp.bfloat16)
        outbound = jnp.dot(placing, mlp_in, preferred_element_type=jnp.float32).astype(jnp.bfloat16)
        outbound = outbound.reshape(expert_count, slot_cap, model_width)
        batch = lax.all_to_all(outbound, "replica", split_axis=0, concat_axis=0, tiled=True)
        source_count = batch.shape[0]
        slot_count = batch.shape[1]
        flat_in = batch.reshape(source_count * slot_count, batch.shape[2])
        gate_part = jnp.dot(flat_in, gate_up[0], preferred_element_type=jnp.float32)
        up_part = jnp.dot(flat_in, gate_up[1], preferred_element_type=jnp.float32)
        hidden = (jax.nn.silu(gate_part) * up_part).astype(jnp.bfloat16)
        partial_out = jnp.dot(hidden, down_weight, preferred_element_type=jnp.float32).reshape(
            source_count, slot_count, model_width
        )
        summed = lax.psum(partial_out.astype(jnp.bfloat16), "expert")
        returned = lax.all_to_all(summed, "replica", split_axis=0, concat_axis=0, tiled=True)
        picked = returned.reshape(expert_count * slot_cap, model_width)[target]
        picked = picked.reshape(row_count, choose_count, model_width).astype(jnp.float32)
        finished = (after_attn.astype(jnp.float32) + jnp.sum(weight[..., None] * picked, 1)).astype(
            jnp.bfloat16
        )
        share_out = lax.dynamic_slice_in_dim(finished, lane_index * share_width, share_width, 1)
        outgoing = finished
        outgoing, share_out, new_entry = (outgoing, share_out, new_entry)
        fresh = jnp.where(active, fresh.at[step_at].set(new_entry), fresh)
        results = jnp.where(active, results.at[step_at].set(share_out), results)
        if tick_index + 1 < tick_total:
            incoming = shifted_2(outgoing, "section", 1)
    return (results[None], fresh[None])


def solution(mesh):
    return jax.shard_map(
        local,
        mesh=mesh,
        in_specs=(
            P(None, "replica", None),
            P("section", None),
            P("section", None, "expert"),
            P("section", None, "expert", None),
            P("section", "expert"),
            P("section", "expert", None),
            P("section", None),
            P("section", None, None),
            P("section", "replica", None, None, "expert"),
            P("section", "replica", "expert", None),
            P("section", "replica", None, "expert", None),
            P("replica", None),
            P("replica"),
            P("section", None, "replica", None),
        ),
        out_specs=(
            P("section", None, "replica", "expert"),
            P("section", None, "replica", "expert", None),
        ),
        check_vma=False,
    )
```

profile of v0, /device:TPU:7, one launch (start us, length us, event | category | flops | bytes accessed | tf_op | source)
XLA Modules:
  0.0 1151.1 jit_solution(12323026308020968581)
XLA Ops:
  8.1 8.7 collective-permute-start
  28.9 1.9 collective-permute-start.1
  31.6 7.0 collective-permute-done.1
  42.6 38.7 %psum.84 = bf16[16,1536]{1,0:T(8,128)(2,1)S(1)} all-reduce(bf16[16,1536]{1,0:T(8,128)(2,1)S(1)} %convolution_convert_fusion.17), channel_id=1, replica_groups=mesh['section'=4,'replica'=16,'expert'=8] {'expert'}, use_global_device_ids=true, to_apply=%region_7.8 | all-reduce | flops 24576 | bytes 98304 | tf_op jit(solution)/shard_map/psum | solution.py:159
  82.6 3.6 all-to-all-start
  86.9 9.2 all-to-all-done
  101.9 97.8 %all-reduce.7.cloned.1.call-done = bf16[16,5,1536]{2,0,1:T(8,128)(2,1)} async-done(((bf16[16,5,1536]{2,0,1:T(8,128)(2,1)}), bf16[16,5,1536]{2,0,1:T(8,128)(2,1)}) %all-reduce.7.cloned.1.call-update) | async-done | bytes 245776 | tf_op jit(solution)/shard_map/psum | solution.py:189
  199.7 1.8 copy.261
  201.5 6.3 all-to-all-start.1
  210.9 9.4 all-to-all-done.1
  226.7 3.8 collective-permute-done.2
  237.1 34.8 %psum.86 = bf16[16,1536]{1,0:T(8,128)(2,1)S(1)} all-reduce(bf16[16,1536]{1,0:T(8,128)(2,1)S(1)} %convolution_convert_fusion.16), channel_id=1, replica_groups=mesh['section'=4,'replica'=16,'expert'=8] {'expert'}, use_global_device_ids=true, to_apply=%region_23.24 | all-reduce | flops 24576 | bytes 98304 | tf_op jit(solution)/shard_map/psum | solution.py:159
  273.9 3.9 all-to-all-start.2
  278.7 11.1 all-to-all-done.2
  295.5 91.9 %all-reduce.9.cloned.1.call-done = bf16[16,5,1536]{2,0,1:T(8,128)(2,1)} async-done(((bf16[16,5,1536]{2,0,1:T(8,128)(2,1)}), bf16[16,5,1536]{2,0,1:T(8,128)(2,1)}) %all-reduce.9.cloned.1.call-update) | async-done | bytes 245776 | tf_op jit(solution)/shard_map/psum | solution.py:189
  389.3 6.3 all-to-all-start.3
  398.7 9.4 all-to-all-done.3
  414.2 4.0 collective-permute-done.3
  422.1 34.8 %psum.88 = bf16[16,1536]{1,0:T(8,128)(2,1)S(1)} all-reduce(bf16[16,1536]{1,0:T(8,128)(2,1)S(1)} %convolution_convert_fusion.15), channel_id=1, replica_groups=mesh['section'=4,'replica'=16,'expert'=8] {'expert'}, use_global_device_ids=true, to_apply=%region_39.40 | all-reduce | flops 24576 | bytes 98304 | tf_op jit(solution)/shard_map/psum | solution.py:159
  458.3 3.9 all-to-all-start.4
  462.8 11.3 all-to-all-done.4
  479.4 92.2 %all-reduce.11.cloned.1.call-done = bf16[16,5,1536]{2,0,1:T(8,128)(2,1)} async-done(((bf16[16,5,1536]{2,0,1:T(8,128)(2,1)}), bf16[16,5,1536]{2,0,1:T(8,128)(2,1)}) %all-reduce.11.cloned.1.call-update) | async-done | bytes 245776 | tf_op jit(solution)/shard_map/psum | solution.py:189
  571.6 1.8 copy.283
  573.5 6.3 all-to-all-start.5
  583.5 8.8 all-to-all-done.5
  598.9 3.5 collective-permute-done.4
  606.3 34.8 %psum.90 = bf16[16,1536]{1,0:T(8,128)(2,1)S(1)} all-reduce(bf16[16,1536]{1,0:T(8,128)(2,1)S(1)} %convolution_convert_fusion.14), channel_id=1, replica_groups=mesh['section'=4,'replica'=16,'expert'=8] {'expert'}, use_global_device_ids=true, to_apply=%region_55.56 | all-reduce | flops 24576 | bytes 98304 | tf_op jit(solution)/shard_map/psum | solution.py:159
  642.4 3.9 all-to-all-start.6
  647.2 11.1 all-to-all-done.6
  664.0 91.9 %all-reduce.13.cloned.1.call-done = bf16[16,5,1536]{2,0,1:T(8,128)(2,1)} async-done(((bf16[16,5,1536]{2,0,1:T(8,128)(2,1)}), bf16[16,5,1536]{2,0,1:T(8,128)(2,1)}) %all-reduce.13.cloned.1.call-update) | async-done | bytes 245776 | tf_op jit(solution)/shard_map/psum | solution.py:189
  755.9 1.8 copy.294
  757.8 6.3 all-to-all-start.7
  767.2 9.4 all-to-all-done.7
  783.2 3.5 collective-permute-done.5
  790.6 34.8 %psum.92 = bf16[16,1536]{1,0:T(8,128)(2,1)S(1)} all-reduce(bf16[16,1536]{1,0:T(8,128)(2,1)S(1)} %convolution_convert_fusion.13), channel_id=1, replica_groups=mesh['section'=4,'replica'=16,'expert'=8] {'expert'}, use_global_device_ids=true, to_apply=%region_71.72 | all-reduce | flops 24576 | bytes 98304 | tf_op jit(solution)/shard_map/psum | solution.py:159
  826.7 3.9 all-to-all-start.8
  831.5 11.1 all-to-all-done.8
  848.4 91.7 %all-reduce.15.cloned.1.call-done = bf16[16,5,1536]{2,0,1:T(8,128)(2,1)} async-done(((bf16[16,5,1536]{2,0,1:T(8,128)(2,1)}), bf16[16,5,1536]{2,0,1:T(8,128)(2,1)}) %all-reduce.15.cloned.1.call-update) | async-done | bytes 245776 | tf_op jit(solution)/shard_map/psum | solution.py:189
  940.1 1.8 copy.305
  942.0 6.3 all-to-all-start.9
  952.6 8.1 all-to-all-done.9
  967.4 3.5 collective-permute-done.6
  974.7 35.0 %psum.94 = bf16[16,1536]{1,0:T(8,128)(2,1)S(1)} all-reduce(bf16[16,1536]{1,0:T(8,128)(2,1)S(1)} %convolution_convert_fusion.12), channel_id=1, replica_groups=mesh['section'=4,'replica'=16,'expert'=8] {'expert'}, use_global_device_ids=true, to_apply=%region_87.88 | all-reduce | flops 24576 | bytes 98304 | tf_op jit(solution)/shard_map/psum | solution.py:159
  1010.9 3.9 all-to-all-start.10
  1020.7 6.1 all-to-all-done.10
  1030.6 90.5 %all-reduce.17.cloned.1.call-done = bf16[16,5,1536]{2,0,1:T(8,128)(2,1)} async-done(((bf16[16,5,1536]{2,0,1:T(8,128)(2,1)}), bf16[16,5,1536]{2,0,1:T(8,128)(2,1)}) %all-reduce.17.cloned.1.call-update) | async-done | bytes 245776 | tf_op jit(solution)/shard_map/psum | solution.py:189
  1122.9 6.3 all-to-all-start.11
  1130.3 11.3 all-to-all-done.11
  (609 shorter events, 145.3 us)
Async XLA Ops:
  7.2 92.9 %copy-start = (bf16[1,1,256,1536]{3,2,1,0:T(8,128)(2,1)S(1)}, bf16[1,1,256,1536]{3,2,1,0:T(8,128)(2,1)}, u32[]{:S(2)}) copy-start(bf16[1,1,256,1536]{3,2,1,0:T(8,128)(2,1)} %param.59) | copy-start | bytes 2359300
  8.1 19.8 %collective-permute-start = (s32[4,8]{0,1:T(8,128)S(1)}, s32[4,8]{0,1:T(8,128)S(1)}, u32[]{:S(2)}, u32[]{:S(2)}) collective-permute-start(s32[4,8]{0,1:T(8,128)S(1)} %slice.535), channel_id=1, source_target_pairs={{0,120},{8,0},{16,8},{24,16},{32,24},{40,32},{48,40},{56,48},{64,5... | collective-permute-start | bytes 392 | tf_op jit(solution)/shard_map/ppermute | solution.py:16
  20.3 66.6 %copy-start.52 = (s32[1,1,16,4]{2,3,1,0:T(4,128)}, s32[1,1,16,4]{2,3,1,0:T(4,128)S(1)}, u32[]{:S(2)}) copy-start(s32[1,1,16,4]{2,3,1,0:T(4,128)S(1)} %get-tuple-element.289) | copy-start | bytes 772
  25.9 182.5 %copy-start.16 = (bf16[3,16,1,128]{3,1,2,0:T(8,128)(2,1)}, bf16[3,16,1,128]{3,1,2,0:T(8,128)(2,1)S(1)}, u32[]{:S(2)}) copy-start(bf16[3,16,1,128]{3,1,2,0:T(8,128)(2,1)S(1)} %constant_dynamic-update-slice_fusion.11) | copy-start | bytes 36868
  28.9 9.7 collective-permute-start.1
  81.5 127.5 %copy-start.15 = (bf16[16,1536]{1,0:T(8,128)(2,1)}, bf16[16,1536]{1,0:T(8,128)(2,1)S(1)}, u32[]{:S(2)}) copy-start(bf16[16,1536]{1,0:T(8,128)(2,1)S(1)} %get-tuple-element.245) | copy-start | bytes 147460
  82.6 13.5 %all-to-all-start = ((bf16[16,5,1536]{2,1,0:T(8,128)(2,1)}), bf16[16,5,1536]{2,1,0:T(8,128)(2,1)S(1)}, u32[]{:S(2)}, u32[]{:S(2)}) async-start(bf16[16,5,1536]{2,1,0:T(8,128)(2,1)} %reshape.2989), calls=%async_computation | async-start | bytes 786432 | tf_op jit(solution)/shard_map/all_to_all | solution.py:179
  86.2 113.5 %all-reduce.7.cloned.1.call-start = ((), (), s32[]{:S(2)}) async-start(), calls=%async_computation.12 | async-start | bytes 491520 | tf_op jit(solution)/shard_map/psum | solution.py:189
  201.5 18.7 %all-to-all-start.1 = ((bf16[16,5,1536]{2,1,0:T(8,128)(2,1)}), bf16[16,5,1536]{2,1,0:T(8,128)(2,1)S(1)}, u32[]{:S(2)}, u32[]{:S(2)}) async-start(bf16[16,5,1536]{2,1,0:T(8,128)(2,1)} %copy.261), calls=%async_computation.1 | async-start | bytes 786432 | tf_op jit(solution)/shard_map/all_to_all | solution.py:190
  224.9 5.7 collective-permute-start.2
  236.6 41.5 %copy-start.50 = (s32[1,1,16,4]{2,3,1,0:T(4,128)S(1)}, s32[1,1,16,4]{2,3,1,0:T(4,128)}, u32[]{:S(2)}) copy-start(s32[1,1,16,4]{2,3,1,0:T(4,128)} %get-tuple-element.287) | copy-start | bytes 772
  236.8 41.8 %copy-start.86 = (s32[64]{0:T(128)S(1)}, s32[64]{0:T(128)}, u32[]{:S(2)}) copy-start(s32[64]{0:T(128)} %copy-done.85) | copy-start | bytes 772
  272.1 125.5 %copy-start.13 = (bf16[16,1536]{1,0:T(8,128)(2,1)}, bf16[16,1536]{1,0:T(8,128)(2,1)S(1)}, u32[]{:S(2)}) copy-start(bf16[16,1536]{1,0:T(8,128)(2,1)S(1)} %get-tuple-element.239) | copy-start | bytes 147460
  273.9 15.9 %all-to-all-start.2 = ((bf16[16,5,1536]{2,1,0:T(8,128)(2,1)}), bf16[16,5,1536]{2,1,0:T(8,128)(2,1)S(1)}, u32[]{:S(2)}, u32[]{:S(2)}) async-start(bf16[16,5,1536]{2,1,0:T(8,128)(2,1)} %reshape.2996), calls=%async_computation.2 | async-start | bytes 786432 | tf_op jit(solution)/shard_map/all_to_all | solution.py:179
  277.9 109.6 %all-reduce.9.cloned.1.call-start = ((), (), s32[]{:S(2)}) async-start(), calls=%async_computation.13 | async-start | bytes 491520 | tf_op jit(solution)/shard_map/psum | solution.py:189
  293.7 102.4 %copy-start.83 = (s32[4]{0:T(128)S(1)}, s32[4]{0:T(128)}, u32[]{:S(2)}) copy-start(s32[4]{0:T(128)} %constant.446.clone.1) | copy-start | bytes 52
  293.7 103.9 %copy-start.104 = (bf16[1,1536,16]{1,2,0:T(8,128)(2,1)S(1)}, bf16[1,1536,16]{1,2,0:T(8,128)(2,1)}, u32[]{:S(2)}) copy-start(bf16[1,1536,16]{1,2,0:T(8,128)(2,1)} %param.57) | copy-start | bytes 147460
  293.7 104.1 %copy-start.53 = (s32[1,1,16,4]{2,3,1,0:T(4,128)S(1)}, s32[1,1,16,4]{2,3,1,0:T(4,128)}, u32[]{:S(2)}) copy-start(s32[1,1,16,4]{2,3,1,0:T(4,128)} %copy-done.52) | copy-start | bytes 772
  389.3 18.7 %all-to-all-start.3 = ((bf16[16,5,1536]{2,1,0:T(8,128)(2,1)}), bf16[16,5,1536]{2,1,0:T(8,128)(2,1)S(1)}, u32[]{:S(2)}, u32[]{:S(2)}) async-start(bf16[16,5,1536]{2,1,0:T(8,128)(2,1)} %copy.272), calls=%async_computation.3 | async-start | bytes 786432 | tf_op jit(solution)/shard_map/all_to_all | solution.py:190
  412.7 5.6 collective-permute-start.3
  457.1 124.5 %copy-start.14 = (bf16[16,1536]{1,0:T(8,128)(2,1)}, bf16[16,1536]{1,0:T(8,128)(2,1)S(1)}, u32[]{:S(2)}) copy-start(bf16[16,1536]{1,0:T(8,128)(2,1)S(1)} %get-tuple-element.233) | copy-start | bytes 147460
  458.3 15.9 %all-to-all-start.4 = ((bf16[16,5,1536]{2,1,0:T(8,128)(2,1)}), bf16[16,5,1536]{2,1,0:T(8,128)(2,1)S(1)}, u32[]{:S(2)}, u32[]{:S(2)}) async-start(bf16[16,5,1536]{2,1,0:T(8,128)(2,1)} %reshape.3004), calls=%async_computation.4 | async-start | bytes 786432 | tf_op jit(solution)/shard_map/all_to_all | solution.py:179
  462.2 109.4 %all-reduce.11.cloned.1.call-start = ((), (), s32[]{:S(2)}) async-start(), calls=%async_computation.14 | async-start | bytes 491520 | tf_op jit(solution)/shard_map/psum | solution.py:189
  478.0 104.5 %copy-start.51 = (s32[1,1,16,4]{2,3,1,0:T(4,128)S(1)}, s32[1,1,16,4]{2,3,1,0:T(4,128)}, u32[]{:S(2)}) copy-start(s32[1,1,16,4]{2,3,1,0:T(4,128)} %get-tuple-element.287) | copy-start | bytes 772
  479.2 104.2 %copy-start.93 = (s32[64]{0:T(128)}, s32[64]{0:T(128)S(1)}, u32[]{:S(2)}) copy-start(s32[64]{0:T(128)S(1)} %select_reduce_fusion.4) | copy-start | bytes 772
  573.5 18.7 %all-to-all-start.5 = ((bf16[16,5,1536]{2,1,0:T(8,128)(2,1)}), bf16[16,5,1536]{2,1,0:T(8,128)(2,1)S(1)}, u32[]{:S(2)}, u32[]{:S(2)}) async-start(bf16[16,5,1536]{2,1,0:T(8,128)(2,1)} %copy.283), calls=%async_computation.5 | async-start | bytes 786432 | tf_op jit(solution)/shard_map/all_to_all | solution.py:190
  596.9 5.6 collective-permute-start.4
  641.2 124.8 %copy-start.12 = (bf16[16,1536]{1,0:T(8,128)(2,1)}, bf16[16,1536]{1,0:T(8,128)(2,1)S(1)}, u32[]{:S(2)}) copy-start(bf16[16,1536]{1,0:T(8,128)(2,1)S(1)} %get-tuple-element.227) | copy-start | bytes 147460
  642.4 15.9 %all-to-all-start.6 = ((bf16[16,5,1536]{2,1,0:T(8,128)(2,1)}), bf16[16,5,1536]{2,1,0:T(8,128)(2,1)S(1)}, u32[]{:S(2)}, u32[]{:S(2)}) async-start(bf16[16,5,1536]{2,1,0:T(8,128)(2,1)} %reshape.3012), calls=%async_computation.6 | async-start | bytes 786432 | tf_op jit(solution)/shard_map/all_to_all | solution.py:179
  646.4 109.6 %all-reduce.13.cloned.1.call-start = ((), (), s32[]{:S(2)}) async-start(), calls=%async_computation.15 | async-start | bytes 491520 | tf_op jit(solution)/shard_map/psum | solution.py:189
  662.2 102.5 %copy-start.84 = (s32[4]{0:T(128)S(1)}, s32[4]{0:T(128)}, u32[]{:S(2)}) copy-start(s32[4]{0:T(128)} %constant.446.clone.1) | copy-start | bytes 52
  662.2 103.9 %copy-start.105 = (bf16[1,1536,16]{1,2,0:T(8,128)(2,1)S(1)}, bf16[1,1536,16]{1,2,0:T(8,128)(2,1)}, u32[]{:S(2)}) copy-start(bf16[1,1536,16]{1,2,0:T(8,128)(2,1)} %param.57) | copy-start | bytes 147460
  662.2 104.0 %copy-start.49 = (s32[1,1,16,4]{2,3,1,0:T(4,128)S(1)}, s32[1,1,16,4]{2,3,1,0:T(4,128)}, u32[]{:S(2)}) copy-start(s32[1,1,16,4]{2,3,1,0:T(4,128)} %get-tuple-element.285) | copy-start | bytes 772
  757.8 18.7 %all-to-all-start.7 = ((bf16[16,5,1536]{2,1,0:T(8,128)(2,1)}), bf16[16,5,1536]{2,1,0:T(8,128)(2,1)S(1)}, u32[]{:S(2)}, u32[]{:S(2)}) async-start(bf16[16,5,1536]{2,1,0:T(8,128)(2,1)} %copy.294), calls=%async_computation.7 | async-start | bytes 786432 | tf_op jit(solution)/shard_map/all_to_all | solution.py:190
  781.2 5.6 collective-permute-start.5
  825.5 125.2 %copy-start.11 = (bf16[16,1536]{1,0:T(8,128)(2,1)}, bf16[16,1536]{1,0:T(8,128)(2,1)S(1)}, u32[]{:S(2)}) copy-start(bf16[16,1536]{1,0:T(8,128)(2,1)S(1)} %get-tuple-element.221) | copy-start | bytes 147460
  826.7 15.9 %all-to-all-start.8 = ((bf16[16,5,1536]{2,1,0:T(8,128)(2,1)}), bf16[16,5,1536]{2,1,0:T(8,128)(2,1)S(1)}, u32[]{:S(2)}, u32[]{:S(2)}) async-start(bf16[16,5,1536]{2,1,0:T(8,128)(2,1)} %reshape.3020), calls=%async_computation.8 | async-start | bytes 786432 | tf_op jit(solution)/shard_map/all_to_all | solution.py:179
  830.6 109.5 %all-reduce.15.cloned.1.call-start = ((), (), s32[]{:S(2)}) async-start(), calls=%async_computation.16 | async-start | bytes 491520 | tf_op jit(solution)/shard_map/psum | solution.py:189
  846.5 102.3 %copy-start.65 = (s32[1,1,16,4]{2,3,1,0:T(4,128)S(1)}, s32[1,1,16,4]{2,3,1,0:T(4,128)}, u32[]{:S(2)}) copy-start(s32[1,1,16,4]{2,3,1,0:T(4,128)} %get-tuple-element.214) | copy-start | bytes 772
  846.5 105.3 %copy-start.47 = (s32[1,1,16,4]{2,3,1,0:T(4,128)S(1)}, s32[1,1,16,4]{2,3,1,0:T(4,128)}, u32[]{:S(2)}) copy-start(s32[1,1,16,4]{2,3,1,0:T(4,128)} %get-tuple-element.293) | copy-start | bytes 772
  942.0 18.7 %all-to-all-start.9 = ((bf16[16,5,1536]{2,1,0:T(8,128)(2,1)}), bf16[16,5,1536]{2,1,0:T(8,128)(2,1)S(1)}, u32[]{:S(2)}, u32[]{:S(2)}) async-start(bf16[16,5,1536]{2,1,0:T(8,128)(2,1)} %copy.305), calls=%async_computation.9 | async-start | bytes 786432 | tf_op jit(solution)/shard_map/all_to_all | solution.py:190
  965.3 5.6 collective-permute-start.6
  974.7 52.2 %copy-start.103 = (bf16[1,1,2,1536,256]{4,3,2,1,0:T(8,128)(2,1)S(1)}, bf16[1,1,2,1536,256]{4,3,2,1,0:T(8,128)(2,1)}, u32[]{:S(2)}) copy-start(bf16[1,1,2,1536,256]{4,3,2,1,0:T(8,128)(2,1)} %param.58) | copy-start | bytes 4718596
  1010.9 15.9 %all-to-all-start.10 = ((bf16[16,5,1536]{2,1,0:T(8,128)(2,1)}), bf16[16,5,1536]{2,1,0:T(8,128)(2,1)S(1)}, u32[]{:S(2)}, u32[]{:S(2)}) async-start(bf16[16,5,1536]{2,1,0:T(8,128)(2,1)} %reshape.3028), calls=%async_computation.10 | async-start | bytes 786432 | tf_op jit(solution)/shard_map/all_to_all | solution.py:179
  1014.8 106.2 %all-reduce.17.cloned.1.call-start = ((), (), s32[]{:S(2)}) async-start(), calls=%async_computation.17 | async-start | bytes 491520 | tf_op jit(solution)/shard_map/psum | solution.py:189
  1027.4 101.7 %copy-start.106 = (bf16[1,1536,16]{1,2,0:T(8,128)(2,1)S(1)}, bf16[1,1536,16]{1,2,0:T(8,128)(2,1)}, u32[]{:S(2)}) copy-start(bf16[1,1536,16]{1,2,0:T(8,128)(2,1)} %param.57) | copy-start | bytes 147460
  1027.5 101.9 %copy-start.45 = (s32[1,1,16,4]{2,3,1,0:T(4,128)S(1)}, s32[1,1,16,4]{2,3,1,0:T(4,128)}, u32[]{:S(2)}) copy-start(s32[1,1,16,4]{2,3,1,0:T(4,128)} %get-tuple-element.215) | copy-start | bytes 772
  1122.9 18.7 %all-to-all-start.11 = ((bf16[16,5,1536]{2,1,0:T(8,128)(2,1)}), bf16[16,5,1536]{2,1,0:T(8,128)(2,1)S(1)}, u32[]{:S(2)}, u32[]{:S(2)}) async-start(bf16[16,5,1536]{2,1,0:T(8,128)(2,1)} %copy.316), calls=%async_computation.11 | async-start | bytes 786432 | tf_op jit(solution)/shard_map/all_to_all | solution.py:190
  (89 other events, 1440.5 us)
Sparse Core Ops, SparseCore 0:
  101.2 98.4 all-reduce.6
  294.9 92.5 all-reduce.8
  479.2 92.4 all-reduce.10
  663.3 92.5 all-reduce.12
  847.6 92.4 all-reduce.14
  1028.6 92.4 all-reduce.16
where the time goes:
time: 1160 us; the launch traced here: 1150 us
  waiting for transfers between devices  698 us (60%)
  blocking collectives  213 us (18%)
  starting transfers between devices  78.5 us (7%)
  other arithmetic  52.9 us (5%)
  local copies, waits for them, and re-layouts  50.7 us (4%)
  matrix products  41.9 us (4%)
  between operations  16.2 us (1%)
    psum x6, waiting for transfers between devices, local(): summed = lax.psum(partial_out.astype(jnp.bfloat16), 'expert')  556 us
    psum x6, blocking collectives, local(): lax.psum(jnp.dot(attended, out_weight, preferred_element_type=jnp.float32...  213 us
    all_to_all x6, waiting for transfers between devices, local(): lax.all_to_all(outbound, 'replica', split_axis=0, concat_axis=0, tiled=True)  60 us
    all_to_all x6, waiting for transfers between devices, local(): lax.all_to_all(summed, 'replica', split_axis=0, concat_axis=0, tiled=True)  56.2 us
    all_to_all x6, starting transfers between devices, local(): lax.all_to_all(summed, 'replica', split_axis=0, concat_axis=0, tiled=True)  37.6 us
    all_to_all x6, starting transfers between devices, local(): lax.all_to_all(outbound, 'replica', split_axis=0, concat_axis=0, tiled=True)  23.2 us
  transfers between devices with their start and end apart: 25, of which 24 were waited for; matrix products, arithmetic and copies ran while one was open for 4% of the time, Pallas kernels for 0%

commit v1 on v0

v1 whole, which is shorter than its diff:
```python
import math

import jax
import jax.numpy as jnp
from jax import lax
from jax.experimental import pallas as pl
from jax.experimental.pallas import tpu as pltpu
from jax.sharding import PartitionSpec as P

MESH = pl.DeviceIdType.MESH
F32 = jnp.float32
BF16 = jnp.bfloat16
EPS = 1e-05
THETA = 150000.0
NEG = -1e30
T = 3
R = 16
D = 1536
H = 768
CW = 256
NR = 16
NZ = 4
SLOT = 5
MIG = 4
NB = 8
NS = 4

ORDER = (
    ("I", 0), ("A", 0), ("B", 0), ("I", 1), ("A", 1), ("I", 2), ("B", 1), ("A", 2),
    ("C", 0), ("B", 2), ("D", 0), ("C", 1), ("E", 0), ("F", 0), ("C", 2), ("G", 0),
    ("E", 1), ("D", 1), ("F", 1), ("E", 2), ("G", 1), ("D", 2), ("H", 0), ("F", 2),
    ("G", 2), ("S", 0), ("S", 1), ("H", 1), ("S", 2), ("H", 2),
)


def iota(shape, axis):
    return lax.broadcasted_iota(jnp.int32, shape, axis).astype(F32)


def div(value, by):
    return jnp.floor((value + 0.5) * (1.0 / by))


def mod(value, by):
    return value - by * div(value, by)


def dot(a, b):
    return jnp.dot(a, b, preferred_element_type=F32)


def dot_t(a, b):
    return lax.dot_general(a, b, (((1,), (1,)), ((), ())), preferred_element_type=F32)


def one_hot(cond):
    return jnp.where(cond, 1.0, 0.0).astype(BF16)


def kernel(
    tok, again, wq, wkv, sinks, wout, fgain, router, wgu, wdown, pool, table_v, table_s, lens, ids,
    out, fresh_out,
    wqkv_v, wout_v, wgu_v, wdown_v, pool_v, cache, leave, next_v, next_s,
    xb, xf, q4, fresh, rope_c, rope_s, bias,
    fold, rep, sel, pack, place, mask_t, comb,
    apo, asend, arecv, ar, h1, hx, disp, recv, yo, ysend, yrecv, rsend, rrecv, psend, xin, bsend, brecv, qp, fin,
    wsem, tsem, msem, ssend, srecv,
):
    s = lax.axis_index("section")
    r = lax.axis_index("replica")
    e = lax.axis_index("expert")
    c = lax.rem(e, 2)
    zh = lax.div(e, 2)
    oc = 1 - c
    sib = {"expert": e + 1 - 2 * c}
    after = lax.rem(s + 1, NS)
    before = lax.rem(s + NS - 1, NS)
    r_next = lax.rem(r + 1, NR)
    r_prev = lax.rem(r + NR - 1, NR)
    z_peers = [{"expert": lax.rem(e + 2 * k, 2 * NZ)} for k in range(1, NZ)]
    r_peers = [lax.rem(r + k, NR) for k in range(1, NR)]

    token_copies = [
        pltpu.make_async_copy(tok.at[t, :, pl.ds(h * H, H)], xb.at[t, h], tsem.at[2 * t + h])
        for t in range(T)
        for h in range(2)
    ]

    @pl.when(s == 0)
    def _():
        for copy in token_copies:
            copy.start()

    local = [(pool, pool_v)]
    for h in range(2):
        rows = pl.ds(h * H, H)
        local.append((wq.at[rows], wqkv_v.at[h, :, pl.ds(0, 256)]))
        local.append((wkv.at[rows], wqkv_v.at[h, :, pl.ds(256, 128)]))
    for h in range(2):
        local.append((wout.at[:, pl.ds(h * H, H)], wout_v.at[h]))
    for h in range(2):
        for k in range(2):
            local.append((wgu.at[k, pl.ds(h * H, H)], wgu_v.at[h, :, pl.ds(k * 256, 256)]))
    for h in range(2):
        local.append((wdown.at[:, pl.ds(h * H, H)], wdown_v.at[h]))
    local = [pltpu.make_async_copy(a, b, wsem.at[i]) for i, (a, b) in enumerate(local)]
    for copy in local:
        copy.start()

    barrier = pltpu.get_barrier_semaphore()
    greeted = [sib, *z_peers, *[{"replica": p} for p in r_peers]]
    for k in range(NZ):
        lane = lax.rem(e + 2 * k, 2 * NZ)
        greeted += [{"section": after, "expert": lane}, {"section": before, "expert": lane}]
    for peer in greeted:
        pl.semaphore_signal(barrier, inc=1, device_id=peer, device_id_type=MESH)

    row16 = iota((R, 1), 0)
    length = jnp.zeros((R, 1), F32)
    for i in range(R):
        length = jnp.where(row16 == i, lens[i].astype(F32), length)
    lane = iota((1, 128), 1)
    freq = jnp.exp(mod(lane, 32) * (-2.0 / 64 * math.log(THETA)))
    sign = jnp.where(mod(lane, 64) < 32, -1.0, 1.0)
    for t in range(T):
        angle = (length + float(t)) * freq
        rope_c[t] = jnp.cos(angle)
        rope_s[t] = jnp.sin(angle) * sign
    inside = iota((R, R * 128), 1) - iota((R, R * 128), 0) * 128.0
    bias[...] = jnp.where((inside >= 0) & (inside < length), 0.0, NEG)
    a, b = iota((256, 128), 0), iota((256, 128), 1)
    fold[...] = jnp.where(mod(a, 64) == b, 0.125, 0.0).astype(BF16)
    a, b = iota((128, 256), 0), iota((128, 256), 1)
    rep[...] = one_hot(a - 64 == mod(b, 64))

    def packed_at(q):
        block = div(q, R * SLOT)
        rest = q - block * (R * SLOT)
        source = div(rest, SLOT)
        return source * 16 + block * SLOT + rest - source * SLOT

    sel[...] = one_hot(packed_at(iota((240, 1), 0)) == iota((240, 256), 1))
    pack[...] = one_hot(packed_at(iota((1, 240), 1)) == iota((256, 240), 0))
    spread = one_hot(div(iota((256, NR), 0), 16) == iota((256, NR), 1))
    spread_t = one_hot(div(iota((NR, 256), 1), 16) == iota((NR, 256), 0))
    tile = one_hot(mod(iota((R, 48), 1), 16) == iota((R, 48), 0))
    tile_t = one_hot(mod(iota((48, R), 0), 16) == iota((48, R), 1))
    earlier = one_hot(iota((R, R), 0) < iota((R, R), 1))
    at = mod(iota((256, 48), 0), 16)
    block = div(at, SLOT)
    wants = jnp.where(block == div(iota((256, 48), 1), 16), at - block * SLOT + 1.0, -1.0)
    at_t = mod(iota((48, 256), 1), 16)
    block_t = div(at_t, SLOT)
    wants_t = jnp.where(block_t == div(iota((48, 256), 0), 16), at_t - block_t * SLOT + 1.0, -1.0)
    chosen_rows = []
    for t in range(T):
        named = ids[t].astype(F32)
        hot = jnp.zeros((NR, R), F32)
        for k in range(4):
            hot = jnp.where(named[k : k + 1, :] == iota((NR, R), 0), 1.0, hot)
        code = (hot * (dot(hot.astype(BF16), earlier) + 1.0)).astype(BF16)
        place[t] = one_hot(dot(spread, dot(code, tile).astype(BF16)) == wants)
        code_t = dot_t(tile_t, code)
        mask_t[t] = jnp.where(dot(code_t.astype(BF16), spread_t) == wants_t, 1.0, 0.0)
        chosen_rows.append(jnp.where(code_t[:R] > 0, 1.0, 0.0))

    local[0].wait()
    for i in range((R - MIG) * NB):
        cache[i] = pool_v[table_s[i % NB, i // NB]]
    pl.semaphore_wait(barrier, len(greeted))

    def remote(src, dst, index, device):
        return pltpu.make_async_remote_copy(
            src_ref=src, dst_ref=dst, send_sem=ssend.at[index], recv_sem=srecv.at[index],
            device_id=device, device_id_type=MESH,
        )

    table_copy = remote(table_v, next_v, 0, {"replica": r_prev})
    table_copy.start()

    def gain_half(gain, h):
        return jnp.where(h == 0, gain[:, :H], gain[:, H:])

    def attn_half(t, h):
        x = xb[t, h].astype(F32) * gain_half(again, h)
        return dot(x.astype(BF16), wqkv_v[h])

    def attn_in(t):
        x = jnp.concatenate([xb[t, 0], xb[t, 1]], axis=1).astype(F32)
        scale = lax.rsqrt(jnp.mean(x * x, axis=-1, keepdims=True) + EPS)
        qkv = (qp[t] + attn_half(t, oc)) * scale
        cosine, sine = rope_c[t], rope_s[t]

        def turned(v):
            width = v.shape[1]
            low = mod(iota((R, width), 1), 64) < 32
            return jnp.where(low, pltpu.roll(v, width - 32, 1), pltpu.roll(v, 32, 1))

        q = qkv[:, :256]
        q = q * jnp.concatenate([cosine, cosine], 1) + turned(q) * jnp.concatenate([sine, sine], 1)
        kv = qkv[:, 256:]
        keys = iota((R, 128), 1) < 64
        kv = kv * jnp.where(keys, cosine, 1.0) + jnp.where(keys, turned(kv) * sine, 0.0)
        fresh[pl.ds(t * R, R)] = kv.astype(BF16)
        fresh_out[t] = kv.astype(BF16)
        q = jnp.concatenate([q] * 4, axis=0)
        head = div(iota((64, 256), 1), 64) == div(iota((64, 256), 0), 16)
        q4[t] = dot(jnp.where(head, q, 0.0).astype(BF16), fold[...]).astype(BF16)

    def attend(t):
        q = q4[t]
        past = cache[...].reshape(R * 128, 128)
        new = fresh[pl.ds(0, R * (t + 1))]
        score = dot_t(q, past)
        score = jnp.concatenate([score[g * R : g * R + R] + bias[...] for g in range(4)], axis=0)
        recent = dot_t(q, new)
        width = R * (t + 1)
        same = mod(iota((64, width), 1), 16) == mod(iota((64, width), 0), 16)
        recent = jnp.where(same, recent, NEG)
        group = div(iota((64, 1), 0), 16)
        sink = jnp.zeros((64, 1), F32)
        for g in range(4):
            sink = jnp.where(group == g, sinks[0, g], sink)
        peak = jnp.maximum(jnp.max(score, -1, keepdims=True), jnp.max(recent, -1, keepdims=True))
        peak = jnp.maximum(peak, sink)
        past_w = jnp.exp(score - peak)
        new_w = jnp.exp(recent - peak)
        total = jnp.sum(past_w, -1, keepdims=True) + jnp.sum(new_w, -1, keepdims=True)
        share = 1.0 / (total + jnp.exp(sink - peak))
        merged = dot((past_w * share).astype(BF16), past) + dot((new_w * share).astype(BF16), new)
        wide = dot(merged.astype(BF16), rep[...])
        head = div(iota((64, 256), 1), 64) == div(iota((64, 256), 0), 16)
        wide = jnp.where(head, wide, 0.0)
        wide = wide[:R] + wide[R : 2 * R] + wide[2 * R : 3 * R] + wide[3 * R :]
        wide = wide.astype(BF16)
        asend[t] = dot(wide, wout_v[oc]).astype(BF16)
        remote(asend.at[t], arecv.at[t], 10 + t, sib).start()
        apo[t] = dot(wide, wout_v[c])

    def pair_sum(t):
        remote(asend.at[t], arecv.at[t], 10 + t, sib).wait_recv()
        ar[t, zh] = (apo[t] + arecv[t].astype(F32)).astype(BF16)
        for peer in z_peers:
            remote(ar.at[t, zh], ar.at[t, zh], 13 + t, peer).start()

    def wait_blocks(ref, sem):
        pltpu.make_async_copy(ref, ref, sem).wait()

    def all_sum(t):
        wait_blocks(ar.at[t, pl.ds(0, NZ - 1)], srecv.at[13 + t])
        total = xb[t, c].astype(F32) + (
            ar[t, 0].astype(F32) + ar[t, 1].astype(F32) + (ar[t, 2].astype(F32) + ar[t, 3].astype(F32))
        )
        half = total.astype(BF16)
        h1[t, c] = half
        remote(h1.at[t, c], h1.at[t, c], 16 + t, sib).start()
        stack = jnp.concatenate([half[:, i * CW : i * CW + CW] for i in range(3)], axis=0)
        disp[t] = dot(place[t], stack).astype(BF16).reshape(NR, 16, CW)
        for peer in r_peers:
            remote(disp.at[t, peer], recv.at[t, c, r], 22 + t, {"replica": peer}).start()
        recv[t, c, r] = disp[t, r]

        @pl.when(s < NS - 1)
        def _():
            remote(h1.at[t, c], hx.at[t], 19 + t, {"section": after}).start()

    def shares(t):
        remote(h1.at[t, c], h1.at[t, c], 16 + t, sib).wait_recv()
        x = jnp.concatenate([h1[t, 0], h1[t, 1]], axis=1).astype(F32)
        scale = lax.rsqrt(jnp.mean(x * x, axis=-1, keepdims=True) + EPS)
        normal = (x * scale * fgain[...]).astype(BF16)
        gates = chosen_rows[t] / (1.0 + jnp.exp(-dot_t(normal, router[...])))
        share = gates / jnp.sum(gates, -1, keepdims=True)
        share = jnp.concatenate([share] * 3, axis=0)
        high = share.astype(BF16)
        low = (share - high.astype(F32)).astype(BF16)
        comb[t, 0] = (dot(high, spread_t) * mask_t[t]).astype(BF16)
        comb[t, 1] = (dot(low, spread_t) * mask_t[t]).astype(BF16)

    def relay(t):
        wait_blocks(recv.at[t, 0, pl.ds(0, NR - 1)], srecv.at[22 + t])
        remote(recv.at[t, c], recv.at[t, c], 25 + t, sib).start()

    def expert(t):
        def half(h):
            rows = dot(sel[...], recv[t, h].reshape(256, CW))
            rows = jnp.concatenate([rows[i * 80 : i * 80 + 80] for i in range(3)], axis=1)
            square = jnp.sum(rows * rows, axis=-1, keepdims=True)
            return square, dot((rows * gain_half(fgain, h)).astype(BF16), wgu_v[h])

        square, both = half(c)
        remote(recv.at[t, c], recv.at[t, c], 25 + t, sib).wait_recv()
        square_o, both_o = half(oc)
        both = (both + both_o) * lax.rsqrt((square + square_o) * (1.0 / D) + EPS)
        gate, up = both[:, :256], both[:, 256:]
        hidden = (gate / (1.0 + jnp.exp(-gate)) * up).astype(BF16)
        ysend[t] = dot(hidden, wdown_v[oc]).astype(BF16)
        remote(ysend.at[t], yrecv.at[t], 28 + t, sib).start()
        yo[t] = dot(hidden, wdown_v[c])

    def give_back(t):
        remote(ysend.at[t], yrecv.at[t], 28 + t, sib).wait_recv()
        y = (yo[t] + yrecv[t].astype(F32)).astype(BF16)
        stack = jnp.concatenate([y[:, i * CW : i * CW + CW] for i in range(3)], axis=0)
        rsend[t] = dot(pack[...], stack).astype(BF16).reshape(NR, 16, CW)
        for peer in r_peers:
            remote(rsend.at[t, peer], rrecv.at[t, r], 31 + t, {"replica": peer}).start()
        rrecv[t, r] = rsend[t, r]

    def combine(t):
        wait_blocks(rrecv.at[t, pl.ds(0, NR - 1)], srecv.at[31 + t])
        rows = rrecv[t].reshape(256, CW)
        got = dot(comb[t, 0], rows) + dot(comb[t, 1], rows)
        psend[t] = jnp.concatenate([got[i * R : i * R + R] for i in range(3)], axis=1).astype(BF16)

        @pl.when(s < NS - 1)
        def _():
            for k in range(NZ):
                peer = {"section": after, "expert": lax.rem(e + 2 * k, 2 * NZ)}
                remote(psend.at[t], xin.at[t, zh], 34 + t, peer).start()

        @pl.when(s == NS - 1)
        def _():
            for peer in z_peers:
                remote(psend.at[t], fin.at[t, zh], 43 + t, peer).start()
            fin[t, zh] = psend[t]

    def total_of(first, parts):
        a, b, c_, d = (parts[k].astype(F32) for k in range(NZ))
        return (first.astype(F32) + (a + b + (c_ + d))).astype(BF16)

    def sum_in(t):
        wait_blocks(xin.at[t], srecv.at[34 + t])
        remote(h1.at[t, c], hx.at[t], 19 + t, {"section": after}).wait_recv()
        xb[t, c] = total_of(hx[t], xin.at[t])
        remote(xb.at[t, c], xb.at[t, c], 37 + t, sib).start()
        qp[t] = attn_half(t, c)

    def lane_columns(t, of):
        x = jnp.concatenate([of[t, 0], of[t, 1]], axis=1).astype(F32)
        quarter = jnp.zeros((R, 384), F32)
        for k in range(NZ):
            quarter = jnp.where(zh == k, x[:, k * 384 : k * 384 + 384], quarter)
        return jnp.where(c == 0, quarter[:, :192], quarter[:, 192:])

    def send_result(t):
        own = lane_columns(t, xb)
        bsend[t] = jnp.concatenate([own, jnp.zeros((R, 64), F32)], axis=1).astype(BF16)
        remote(bsend.at[t], brecv.at[t], 40 + t, {"section": before}).start()

    for copy in local[1:5]:
        copy.wait()

    @pl.when(s == 0)
    def _():
        for t in range(T):
            token_copies[2 * t].wait()
            token_copies[2 * t + 1].wait()
            qp[t] = attn_half(t, c)
            attn_in(t)

    table_copy.wait_recv()
    to_smem = pltpu.make_async_copy(next_v, next_s, msem)
    to_smem.start()
    to_smem.wait()
    for i in range(MIG * NB):
        leave[i] = pool_v[next_s[i % NB, R - MIG + i // NB]]
    start = (R - MIG) * NB
    leave_copy = remote(leave, cache.at[pl.ds(start, MIG * NB)], 1, {"replica": r_next})
    leave_copy.start()
    leave_copy.wait_recv()
    for copy in local[5:]:
        copy.wait()

    def on_arrival(t):
        @pl.when(s > 0)
        def _():
            sum_in(t)

    def attention(t):
        @pl.when(s > 0)
        def _():
            remote(xb.at[t, c], xb.at[t, c], 37 + t, sib).wait_recv()
            attn_in(t)

        attend(t)

    def result(t):
        @pl.when(s > 0)
        def _():
            send_result(t)

    steps = {
        "I": on_arrival, "A": attention, "B": pair_sum, "C": all_sum, "D": shares,
        "E": relay, "F": expert, "G": give_back, "H": combine, "S": result,
    }
    for name, t in ORDER:
        steps[name](t)

    @pl.when(s == NS - 1)
    def _():
        for t in range(T):
            wait_blocks(fin.at[t, pl.ds(0, NZ - 1)], srecv.at[43 + t])
            xf[t, c] = total_of(h1[t, c], fin.at[t])
            remote(xf.at[t, c], xf.at[t, c], 46 + t, sib).start()
        for t in range(T):
            remote(xf.at[t, c], xf.at[t, c], 46 + t, sib).wait_recv()
            out[t] = lane_columns(t, xf).astype(BF16)

    @pl.when(s < NS - 1)
    def _():
        for t in range(T):
            remote(bsend.at[t], brecv.at[t], 40 + t, {"section": before}).wait_recv()
            out[t] = brecv[t][:, :192]

    table_copy.wait_send()
    leave_copy.wait_send()

    def left(t, pairs):
        for index, ref in pairs:
            wait_blocks(ref, ssend.at[index + t])

    for t in range(T):
        left(t, (
            (10, asend.at[t]),
            (13, ar.at[t, pl.ds(0, NZ - 1)]),
            (16, h1.at[t, c]),
            (22, disp.at[t, pl.ds(0, NR - 1)]),
            (25, recv.at[t, c]),
            (28, ysend.at[t]),
            (31, rsend.at[t, pl.ds(0, NR - 1)]),
        ))

    @pl.when(s > 0)
    def _():
        for t in range(T):
            left(t, ((37, xb.at[t, c]), (40, bsend.at[t])))

    @pl.when(s < NS - 1)
    def _():
        for t in range(T):
            left(t, ((19, h1.at[t, c]), (34, xin.at[t])))

    @pl.when(s == NS - 1)
    def _():
        for t in range(T):
            left(t, ((43, fin.at[t, pl.ds(0, NZ - 1)]), (46, xf.at[t, c])))


def local_part(
    tokens, attn_gain, w_query, w_keyval, sinks, w_out, ffn_gain, router, w_gate_up, w_down,
    kv_pool, block_table, lengths, expert_ids,
):
    vmem = pl.BlockSpec(memory_space=pltpu.VMEM)
    smem = pl.BlockSpec(memory_space=pltpu.SMEM)
    hbm = pl.BlockSpec(memory_space=pltpu.HBM)
    table = block_table.T
    operands = [
        (tokens, hbm),
        (attn_gain, vmem),
        (w_query[0], hbm),
        (w_keyval.reshape(D, 128), hbm),
        (sinks, smem),
        (w_out[0], hbm),
        (ffn_gain, vmem),
        (router[0].T, vmem),
        (w_gate_up[0, 0], hbm),
        (w_down[0, 0], hbm),
        (kv_pool.reshape(128, 16, 128), hbm),
        (table, vmem),
        (table, smem),
        (lengths, smem),
        (expert_ids[0].transpose(0, 2, 1), vmem),
    ]
    V = pltpu.VMEM
    scratch = [
        V((2, H, 384), BF16), V((2, 256, H), BF16), V((2, H, 512), BF16), V((2, 256, H), BF16),
        V((128, 16, 128), BF16), V((128, 16, 128), BF16), V((MIG * NB, 16, 128), BF16),
        V((NB, R), jnp.int32), pltpu.SMEM((NB, R), jnp.int32),
        V((T, 2, R, H), BF16), V((T, 2, R, H), BF16), V((T, 64, 128), BF16), V((T * R, 128), BF16),
        V((T, R, 128), F32), V((T, R, 128), F32), V((R, R * 128), F32),
        V((256, 128), BF16), V((128, 256), BF16), V((240, 256), BF16), V((256, 240), BF16),
        V((T, 256, 48), BF16), V((T, 48, 256), F32), V((T, 2, 48, 256), BF16),
        V((T, R, H), F32), V((T, R, H), BF16), V((T, R, H), BF16), V((T, NZ, R, H), BF16),
        V((T, 2, R, H), BF16), V((T, R, H), BF16), V((T, NR, 16, CW), BF16),
        V((T, 2, NR, 16, CW), BF16), V((T, 80, H), F32), V((T, 80, H), BF16), V((T, 80, H), BF16),
        V((T, NR, 16, CW), BF16), V((T, NR, 16, CW), BF16), V((T, R, H), BF16),
        V((T, NZ, R, H), BF16), V((T, R, 256), BF16), V((T, R, 256), BF16),
        V((T, R, 384), F32), V((T, NZ, R, H), BF16),
        pltpu.SemaphoreType.DMA((13,)), pltpu.SemaphoreType.DMA((2 * T,)), pltpu.SemaphoreType.DMA,
        pltpu.SemaphoreType.DMA((49,)), pltpu.SemaphoreType.DMA((49,)),
    ]
    layer_out, fresh = pl.pallas_call(
        kernel,
        out_shape=(
            jax.ShapeDtypeStruct((T, R, 192), BF16),
            jax.ShapeDtypeStruct((T, R, 128), BF16),
        ),
        in_specs=[spec for _, spec in operands],
        out_specs=(vmem, vmem),
        scratch_shapes=scratch,
        compiler_params=pltpu.CompilerParams(
            collective_id=0, has_side_effects=True, vmem_limit_bytes=62 << 20
        ),
        name="layers",
    )(*[value for value, _ in operands])
    return layer_out[None], fresh.reshape(1, T, R, 1, 128)


def solution(mesh):
    return jax.shard_map(
        local_part,
        mesh=mesh,
        in_specs=(
            P(None, "replica", None),
            P("section", None),
            P("section", None, "expert"),
            P("section", None, "expert", None),
            P("section", "expert"),
            P("section", "expert", None),
            P("section", None),
            P("section", None, None),
            P("section", "replica", None, None, "expert"),
            P("section", "replica", "expert", None),
            P("section", "replica", None, "expert", None),
            P("replica", None),
            P("replica"),
            P("section", None, "replica", None),
        ),
        out_specs=(
            P("section", None, "replica", "expert"),
            P("section", None, "replica", "expert", None),
        ),
        check_vma=False,
    )
```

time: 1160 us -> 230 us (0.20)
  waiting for transfers between devices: 698 us -> 0 us
  Pallas kernels: 0 us -> 223 us
  blocking collectives: 213 us -> 0 us
  starting transfers between devices: 78.5 us -> 0 us
  other arithmetic: 52.9 us -> 0 us
  local copies, waits for them, and re-layouts: 50.7 us -> 2.65 us
  matrix products: 41.9 us -> 0 us
  between operations: 16.2 us -> 0.64 us
    psum x6 -> x0, waiting for transfers between devices: 556 us -> none  [local(): summed = lax.psum(partial_out.astype(jnp.bfloat16), 'expert')]
    pallas_call x0 -> x1, Pallas kernels: none -> 223 us  [local_part(): pl.pallas_call(kernel, out_shape=(jax.ShapeDtypeStruct((T, R, 192), BF16)...]
    psum x6 -> x0, blocking collectives: 213 us -> none  [local(): lax.psum(jnp.dot(attended, out_weight, preferred_element_type=jnp.float32...]
    all_to_all x12 -> x0, waiting for transfers between devices: 116 us -> none  [the longest x6 60 us: local(): lax.all_to_all(outbound, 'replica', split_axis=0, concat_axis=0, tiled=True)]
    all_to_all x12 -> x0, starting transfers between devices: 60.8 us -> none  [the longest x6 37.6 us: local(): lax.all_to_all(summed, 'replica', split_axis=0, concat_axis=0, tiled=True)]
    dot_general x72 -> x0, matrix products: 41.9 us -> none  [the longest x6 7.94 us: local(): up_part = jnp.dot(flat_in, gate_up[1], preferred_element_type=jnp.float32)]
    ppermute x7 -> x0, waiting for transfers between devices: 25.4 us -> none  [the longest x5 18.5 us: shifted_2(): lax.ppermute(value, axis, [(source, source + steps) for source in range(l...]
    ppermute x7 -> x0, starting transfers between devices: 17.3 us -> none  [the longest x2 10.6 us: shifted(): lax.ppermute(shard, axis, [(i, (i + by) % length) for i in range(length)])]
  transfers between devices with their start and end apart: 25 -> 0, of which waited for: 24 -> 0; matrix products, arithmetic and copies ran while one was open for 4% -> 0% of each run, Pallas kernels for 0% -> 0%
where the time goes in v1:
time: 230 us; the launch traced here: 226 us
  Pallas kernels  223 us (97%)
  local copies, waits for them, and re-layouts  2.65 us (1%)
    pallas_call x1, Pallas kernels, local_part(): pl.pallas_call(kernel, out_shape=(jax.ShapeDtypeStruct((T, R, 192), BF16)...  223 us

profile of v1, /device:TPU:7, one launch (start us, length us, event | category | flops | bytes accessed | tf_op | source)
XLA Modules:
  0.0 226.4 jit_solution(76282406637307669)
XLA Ops:
  0.6 223.1 %layers.1 = (bf16[3,16,192]{2,1,0:T(8,128)(2,1)}, bf16[3,16,128]{2,1,0:T(8,128)(2,1)}) custom-call(bf16[3,16,1536]{2,1,0:T(8,128)(2,1)} %tok.1, f32[1,1536]{1,0:T(1,128)} %again.1, bf16[1536,256]{1,0:T(8,128)(2,1)} %bitcast.18, bf16[1536,128]{1,0:T(8,128)(2,1)} %bitcast.22, f32[1,4]{1,0:T(1,128)} %sinks.1, bf16[256,1536]{1,0:T(8,128)(2,1)} %bitcast.19, ...), custom_call_target="tpu_custom_call" | custom-call | tf_op jit(solution)/shard_map/layers/pallas_call | solution.py:493
  223.8 1.3 copy.19
  225.1 1.3 copy.20

commit v2 on v1

--- a/solution.py
+++ b/solution.py
@@ -58,9 +58,9 @@
 
 
 def kernel(
-    tok, again, wq, wkv, sinks, wout, fgain, router, wgu, wdown, pool, table_v, table_s, lens, ids,
+    tok, again, wq, wkv, sinks, wout, fgain, router, wgu, wdown, pool, table_s, lens, ids,
     out, fresh_out,
-    wqkv_v, wout_v, wgu_v, wdown_v, pool_v, cache, leave, next_v, next_s,
+    wqkv_v, wout_v, wgu_v, wdown_v, pool_v, cache, leave, came, index_v, index_s,
     xb, xf, q4, fresh, rope_c, rope_s, bias,
     fold, rep, sel, pack, place, mask_t, comb,
     apo, asend, arecv, ar, h1, hx, disp, recv, yo, ysend, yrecv, rsend, rrecv, psend, xin, bsend, brecv, qp, fin,
@@ -77,8 +77,23 @@
     before = lax.rem(s + NS - 1, NS)
     r_next = lax.rem(r + 1, NR)
     r_prev = lax.rem(r + NR - 1, NR)
-    z_peers = [{"expert": lax.rem(e + 2 * k, 2 * NZ)} for k in range(1, NZ)]
+    z_peers = [{"expert": lax.rem(e + 2 * k, 2 * NZ)} for k in (2, 1, 3)]
     r_peers = [lax.rem(r + k, NR) for k in range(1, NR)]
+
+    low = lax.div(r, NR // NZ)
+
+    def hops(start, end):
+        way = lax.rem(end - start + NZ, NZ)
+        half_way = lax.div(way, 2) * (1 - lax.rem(way, 2))
+        return lax.rem(way + 1, NZ) - 1 - NZ * lax.rem(start, 2) * half_way
+
+    def lane_at(z):
+        return 2 * lax.rem(lax.div(z + NZ * NZ, NZ), NZ) + c
+
+    here = NZ * zh + low
+    lane_to = [lane_at(here + hops(low, lax.div(p, NR // NZ))) for p in r_peers]
+    lane_from = [lane_at(here - hops(lax.div(p, NR // NZ), low)) for p in r_peers]
+    r_targets = [(p, {"replica": p, "expert": lane}) for p, lane in zip(r_peers, lane_to)]
 
     token_copies = [
         pltpu.make_async_copy(tok.at[t, :, pl.ds(h * H, H)], xb.at[t, h], tsem.at[2 * t + h])
@@ -108,7 +123,7 @@
         copy.start()
 
     barrier = pltpu.get_barrier_semaphore()
-    greeted = [sib, *z_peers, *[{"replica": p} for p in r_peers]]
+    greeted = [sib, {"replica": r_prev}, *z_peers, *[{"replica": p, "expert": lane} for p, lane in zip(r_peers, lane_from)]]
     for k in range(NZ):
         lane = lax.rem(e + 2 * k, 2 * NZ)
         greeted += [{"section": after, "expert": lane}, {"section": before, "expert": lane}]
@@ -164,9 +179,34 @@
         mask_t[t] = jnp.where(dot(code_t.astype(BF16), spread_t) == wants_t, 1.0, 0.0)
         chosen_rows.append(jnp.where(code_t[:R] > 0, 1.0, 0.0))
 
+    block_id = iota((1, 128), 1)
+    own = jnp.zeros((1, 128), F32)
+    taken = jnp.zeros((1, 128), F32)
+    entry = iota((MIG * NB, 1), 0)
+    entries = jnp.zeros((MIG * NB, 1), F32)
+    for i in range(R * NB):
+        named_block = table_s[i % NB, i // NB].astype(F32)
+        if i < (R - MIG) * NB:
+            own = jnp.where(block_id == named_block, 1.0, own)
+        else:
+            taken = jnp.where(block_id == named_block, 1.0, taken)
+            entries = jnp.where(entry == i - (R - MIG) * NB, named_block, entries)
+    below = one_hot(iota((128, 128), 0) < iota((128, 128), 1))
+    marks = jnp.concatenate([1.0 - own, taken] + [jnp.zeros((1, 128), F32)] * 14, axis=0)
+    ranks = dot(marks.astype(BF16), below)
+    leaves = (ranks[0:1] == entry) & (own == 0)
+    leaving = jnp.sum(jnp.where(leaves, block_id, 0.0), axis=1, keepdims=True)
+    coming = jnp.sum(jnp.where(entries == block_id, ranks[1:2], 0.0), axis=1, keepdims=True)
+    column = iota((MIG * NB, 128), 1)
+    index_v[...] = jnp.where(column == 0, leaving, coming).astype(jnp.int32)
+    to_smem = pltpu.make_async_copy(index_v, index_s, msem)
+    to_smem.start()
     local[0].wait()
     for i in range((R - MIG) * NB):
         cache[i] = pool_v[table_s[i % NB, i // NB]]
+    to_smem.wait()
+    for i in range(MIG * NB):
+        leave[i] = pool_v[jnp.clip(index_s[i, 0], 0, 127)]
     pl.semaphore_wait(barrier, len(greeted))
 
     def remote(src, dst, index, device):
@@ -175,8 +215,8 @@
             device_id=device, device_id_type=MESH,
         )
 
-    table_copy = remote(table_v, next_v, 0, {"replica": r_prev})
-    table_copy.start()
+    leave_copy = remote(leave, came, 1, {"replica": r_next})
+    leave_copy.start()
 
     def gain_half(gain, h):
         return jnp.where(h == 0, gain[:, :H], gain[:, H:])
@@ -256,8 +296,8 @@
         remote(h1.at[t, c], h1.at[t, c], 16 + t, sib).start()
         stack = jnp.concatenate([half[:, i * CW : i * CW + CW] for i in range(3)], axis=0)
         disp[t] = dot(place[t], stack).astype(BF16).reshape(NR, 16, CW)
-        for peer in r_peers:
-            remote(disp.at[t, peer], recv.at[t, c, r], 22 + t, {"replica": peer}).start()
+        for peer, device in r_targets:
+            remote(disp.at[t, peer], recv.at[t, c, r], 22 + t, device).start()
         recv[t, c, r] = disp[t, r]
 
         @pl.when(s < NS - 1)
@@ -303,8 +343,8 @@
         y = (yo[t] + yrecv[t].astype(F32)).astype(BF16)
         stack = jnp.concatenate([y[:, i * CW : i * CW + CW] for i in range(3)], axis=0)
         rsend[t] = dot(pack[...], stack).astype(BF16).reshape(NR, 16, CW)
-        for peer in r_peers:
-            remote(rsend.at[t, peer], rrecv.at[t, r], 31 + t, {"replica": peer}).start()
+        for peer, device in r_targets:
+            remote(rsend.at[t, peer], rrecv.at[t, r], 31 + t, device).start()
         rrecv[t, r] = rsend[t, r]
 
     def combine(t):
@@ -315,7 +355,7 @@
 
         @pl.when(s < NS - 1)
         def _():
-            for k in range(NZ):
+            for k in (2, 1, 3, 0):
                 peer = {"section": after, "expert": lax.rem(e + 2 * k, 2 * NZ)}
                 remote(psend.at[t], xin.at[t, zh], 34 + t, peer).start()
 
@@ -359,18 +399,11 @@
             qp[t] = attn_half(t, c)
             attn_in(t)
 
-    table_copy.wait_recv()
-    to_smem = pltpu.make_async_copy(next_v, next_s, msem)
-    to_smem.start()
-    to_smem.wait()
-    for i in range(MIG * NB):
-        leave[i] = pool_v[next_s[i % NB, R - MIG + i // NB]]
-    start = (R - MIG) * NB
-    leave_copy = remote(leave, cache.at[pl.ds(start, MIG * NB)], 1, {"replica": r_next})
-    leave_copy.start()
-    leave_copy.wait_recv()
     for copy in local[5:]:
         copy.wait()
+    leave_copy.wait_recv()
+    for i in range(MIG * NB):
+        cache[(R - MIG) * NB + i] = came[jnp.clip(index_s[i, 1], 0, MIG * NB - 1)]
 
     def on_arrival(t):
         @pl.when(s > 0)
@@ -413,7 +446,6 @@
             remote(bsend.at[t], brecv.at[t], 40 + t, {"section": before}).wait_recv()
             out[t] = brecv[t][:, :192]
 
-    table_copy.wait_send()
     leave_copy.wait_send()
 
     def left(t, pairs):
@@ -454,7 +486,6 @@
     vmem = pl.BlockSpec(memory_space=pltpu.VMEM)
     smem = pl.BlockSpec(memory_space=pltpu.SMEM)
     hbm = pl.BlockSpec(memory_space=pltpu.HBM)
-    table = block_table.T
     operands = [
         (tokens, hbm),
         (attn_gain, vmem),
@@ -467,8 +498,7 @@
         (w_gate_up[0, 0], hbm),
         (w_down[0, 0], hbm),
         (kv_pool.reshape(128, 16, 128), hbm),
-        (table, vmem),
-        (table, smem),
+        (block_table.T, smem),
         (lengths, smem),
         (expert_ids[0].transpose(0, 2, 1), vmem),
     ]
@@ -476,7 +506,8 @@
     scratch = [
         V((2, H, 384), BF16), V((2, 256, H), BF16), V((2, H, 512), BF16), V((2, 256, H), BF16),
         V((128, 16, 128), BF16), V((128, 16, 128), BF16), V((MIG * NB, 16, 128), BF16),
-        V((NB, R), jnp.int32), pltpu.SMEM((NB, R), jnp.int32),
+        V((MIG * NB, 16, 128), BF16),
+        V((MIG * NB, 128), jnp.int32), pltpu.SMEM((MIG * NB, 128), jnp.int32),
         V((T, 2, R, H), BF16), V((T, 2, R, H), BF16), V((T, 64, 128), BF16), V((T * R, 128), BF16),
         V((T, R, 128), F32), V((T, R, 128), F32), V((R, R * 128), F32),
         V((256, 128), BF16), V((128, 256), BF16), V((240, 256), BF16), V((256, 240), BF16),

time: 230 us -> 206 us (0.90); the launches traced: 226 us -> 205 us
  Pallas kernels: 223 us -> 202 us
    pallas_call x1, Pallas kernels: 223 us -> 202 us  [local_part(): pl.pallas_call(kernel, out_shape=(jax.ShapeDtypeStruct((T, R, 192), BF16)...]
where the time goes in v2:
time: 206 us; the launch traced here: 205 us
  Pallas kernels  202 us (98%)
  local copies, waits for them, and re-layouts  2.65 us (1%)
    pallas_call x1, Pallas kernels, local_part(): pl.pallas_call(kernel, out_shape=(jax.ShapeDtypeStruct((T, R, 192), BF16)...  202 us

profile of v2, /device:TPU:7, one launch (start us, length us, event | category | flops | bytes accessed | tf_op | source)
XLA Modules:
  0.0 205.3 jit_solution(4622757897531382022)
XLA Ops:
  0.6 202.0 %layers.1 = (bf16[3,16,192]{2,1,0:T(8,128)(2,1)}, bf16[3,16,128]{2,1,0:T(8,128)(2,1)}) custom-call(bf16[3,16,1536]{2,1,0:T(8,128)(2,1)} %tok.1, f32[1,1536]{1,0:T(1,128)} %again.1, bf16[1536,256]{1,0:T(8,128)(2,1)} %bitcast.18, bf16[1536,128]{1,0:T(8,128)(2,1)} %bitcast.22, f32[1,4]{1,0:T(1,128)} %sinks.1, bf16[256,1536]{1,0:T(8,128)(2,1)} %bitcast.19, ...), custom_call_target="tpu_custom_call" | custom-call | tf_op jit(solution)/shard_map/layers/pallas_call | solution.py:524
  202.6 1.3 copy.19
  204.0 1.3 copy.20

commit v3 on v2

--- a/solution.py
+++ b/solution.py
@@ -26,10 +26,10 @@
 NS = 4
 
 ORDER = (
-    ("I", 0), ("A", 0), ("B", 0), ("I", 1), ("A", 1), ("I", 2), ("B", 1), ("A", 2),
-    ("C", 0), ("B", 2), ("D", 0), ("C", 1), ("E", 0), ("F", 0), ("C", 2), ("G", 0),
-    ("E", 1), ("D", 1), ("F", 1), ("E", 2), ("G", 1), ("D", 2), ("H", 0), ("F", 2),
-    ("G", 2), ("S", 0), ("S", 1), ("H", 1), ("S", 2), ("H", 2),
+    ("I", 0), ("A", 0), ("B", 0), ("I", 1), ("S", 0), ("A", 1), ("B", 1), ("I", 2),
+    ("A", 2), ("C", 0), ("B", 2), ("C", 1), ("D", 0), ("E", 0), ("D", 1), ("S", 1),
+    ("F", 0), ("C", 2), ("G", 0), ("E", 1), ("S", 2), ("D", 2), ("F", 1), ("G", 1),
+    ("E", 2), ("H", 0), ("F", 2), ("G", 2), ("H", 1), ("H", 2),
 )
 
 

time: 206 us -> 198 us (0.961)
  Pallas kernels: 202 us -> 194 us
    pallas_call x1, Pallas kernels: 202 us -> 194 us  [local_part(): pl.pallas_call(kernel, out_shape=(jax.ShapeDtypeStruct((T, R, 192), BF16)...]
where the time goes in v3:
time: 198 us; the launch traced here: 197 us
  Pallas kernels  194 us (98%)
  local copies, waits for them, and re-layouts  2.65 us (1%)
    pallas_call x1, Pallas kernels, local_part(): pl.pallas_call(kernel, out_shape=(jax.ShapeDtypeStruct((T, R, 192), BF16)...  194 us

profile of v3, /device:TPU:7, one launch (start us, length us, event | category | flops | bytes accessed | tf_op | source)
XLA Modules:
  0.0 197.2 jit_solution(12034327719749019027)
XLA Ops:
  0.6 193.9 %layers.1 = (bf16[3,16,192]{2,1,0:T(8,128)(2,1)}, bf16[3,16,128]{2,1,0:T(8,128)(2,1)}) custom-call(bf16[3,16,1536]{2,1,0:T(8,128)(2,1)} %tok.1, f32[1,1536]{1,0:T(1,128)} %again.1, bf16[1536,256]{1,0:T(8,128)(2,1)} %bitcast.18, bf16[1536,128]{1,0:T(8,128)(2,1)} %bitcast.22, f32[1,4]{1,0:T(1,128)} %sinks.1, bf16[256,1536]{1,0:T(8,128)(2,1)} %bitcast.19, ...), custom_call_target="tpu_custom_call" | custom-call | tf_op jit(solution)/shard_map/layers/pallas_call | solution.py:524
  194.5 1.3 copy.19
  195.9 1.3 copy.20

commit v4 on v3

--- a/solution.py
+++ b/solution.py
@@ -27,9 +27,9 @@
 
 ORDER = (
     ("I", 0), ("A", 0), ("B", 0), ("I", 1), ("S", 0), ("A", 1), ("B", 1), ("I", 2),
-    ("A", 2), ("C", 0), ("B", 2), ("C", 1), ("D", 0), ("E", 0), ("D", 1), ("S", 1),
+    ("C", 0), ("A", 2), ("B", 2), ("C", 1), ("D", 0), ("E", 0), ("D", 1), ("S", 1),
     ("F", 0), ("C", 2), ("G", 0), ("E", 1), ("S", 2), ("D", 2), ("F", 1), ("G", 1),
-    ("E", 2), ("H", 0), ("F", 2), ("G", 2), ("H", 1), ("H", 2),
+    ("H", 0), ("E", 2), ("F", 2), ("G", 2), ("H", 1), ("H", 2),
 )
 
 

time: 198 us -> 195 us (0.985)
  Pallas kernels: 194 us -> 191 us
    pallas_call x1, Pallas kernels: 194 us -> 191 us  [local_part(): pl.pallas_call(kernel, out_shape=(jax.ShapeDtypeStruct((T, R, 192), BF16)...]
where the time goes in v4:
time: 195 us
  Pallas kernels  191 us (98%)
  local copies, waits for them, and re-layouts  2.65 us (1%)
    pallas_call x1, Pallas kernels, local_part(): pl.pallas_call(kernel, out_shape=(jax.ShapeDtypeStruct((T, R, 192), BF16)...  191 us

profile of v4, /device:TPU:7, one launch (start us, length us, event | category | flops | bytes accessed | tf_op | source)
XLA Modules:
  0.0 194.7 jit_solution(5676683427219135962)
XLA Ops:
  0.6 191.4 %layers.1 = (bf16[3,16,192]{2,1,0:T(8,128)(2,1)}, bf16[3,16,128]{2,1,0:T(8,128)(2,1)}) custom-call(bf16[3,16,1536]{2,1,0:T(8,128)(2,1)} %tok.1, f32[1,1536]{1,0:T(1,128)} %again.1, bf16[1536,256]{1,0:T(8,128)(2,1)} %bitcast.18, bf16[1536,128]{1,0:T(8,128)(2,1)} %bitcast.22, f32[1,4]{1,0:T(1,128)} %sinks.1, bf16[256,1536]{1,0:T(8,128)(2,1)} %bitcast.19, ...), custom_call_target="tpu_custom_call" | custom-call | tf_op jit(solution)/shard_map/layers/pallas_call | solution.py:524
  192.0 1.3 copy.19
  193.4 1.3 copy.20
